TPU v7x, 512 devices: a whole 4x8x8 slice. The times are simulated.
512 devices in a mesh: dp: 32 (over x, z_lo, core), fsdp: 16 (over z_hi, y).
Axes of the slice: x: 4, y: 8, z: 8 (z_hi: 2, z_lo: 4; z = z_hi * 4 + z_lo), core: 2. Of those that a mesh axis runs over, the one named last changes fastest.
Arguments:
- hidden: bfloat16 [4096, 1536], P('dp', 'fsdp'), may hold values from -0.5 to 0.5
- teacher: bfloat16 [4096, 4096], P('dp', 'fsdp'), may hold values from -40 to 40
- projector: bfloat16 [1536, 1536], P('fsdp'), may hold values from -0.15625 to 0.15625
Outputs:
- grad_hidden: float32 [4096, 1536], P('dp', 'fsdp')
- grad_proj: float32 [1536, 1536], P('fsdp')
- loss: float32 [], replicated
All inputs are finite; a program needn't handle non-finite values.
Results may differ from a plain program's by a relative error of at most 0.0085.
The roundings to bfloat16 on the way count: a program that leaves them out, or rounds other values in their place, can miss the bound.
Values may be sent and summed in bfloat16 or wider, within the bound.
No kernel may reach another device: no remote copies, remote signals or barrier semaphores. Data moves between devices by JAX's collectives and lax.ppermute only.
A program may use at most 64 MiB of HBM per device.

v0:
```python
import jax
import jax.numpy as jnp
from jax import lax
from jax.sharding import PartitionSpec as P

EPSILON = 1e-06
HIGHEST = lax.Precision.HIGHEST


def radial_sum(unit_f, grad_unit):
    return lax.psum(jnp.sum(unit_f * grad_unit, axis=1), "fsdp")


def body(hidden, teacher, projector):
    row_count = hidden.shape[0]
    width_local = hidden.shape[1]
    contract = (((1,), (1,)), ((), ()))
    rows_first = (((0,), (0,)), ((), ()))
    width_cross = (((0,), (1,)), ((), ()))
    embed = lax.psum_scatter(
        lax.dot_general(projector, hidden, width_cross, preferred_element_type=jnp.float32),
        "fsdp",
        scatter_dimension=0,
        tiled=True,
    ).T
    teach_f = teacher.astype(jnp.float32)
    sq_student, sq_teacher = lax.psum(
        (jnp.sum(embed * embed, axis=1), jnp.sum(teach_f * teach_f, axis=1)), "fsdp"
    )
    inv_student = lax.rsqrt(sq_student + EPSILON)[:, None]
    unit_f = embed * inv_student
    student = unit_f.astype(jnp.bfloat16)
    target = (teach_f * lax.rsqrt(sq_teacher + EPSILON)[:, None]).astype(jnp.bfloat16)
    upper = jnp.concatenate([student, target], axis=1)
    lower = jnp.concatenate([student, -target], axis=1)
    lower_all = lax.all_gather(lower, "dp", axis=0, tiled=True)
    partial_value = lax.dot_general(upper, lower_all, contract, preferred_element_type=jnp.float32)
    differ = lax.psum(partial_value, "fsdp")
    squares = jnp.sum(differ * differ)
    grad_unit = 4.0 * jnp.dot(
        differ,
        lower_all[:, :width_local].astype(jnp.float32),
        precision=HIGHEST,
        preferred_element_type=jnp.float32,
    )
    radial = radial_sum(unit_f, grad_unit)
    grad_embed = (inv_student * (grad_unit - unit_f * radial[:, None])).astype(jnp.bfloat16)
    piece = lax.all_gather(grad_embed, "fsdp", axis=1, tiled=True)
    hidden_acc = lax.dot_general(piece, projector, contract, preferred_element_type=jnp.float32)
    proj_piece = lax.dot_general(hidden, piece, rows_first, preferred_element_type=jnp.float32)
    grad_proj, squares_all = lax.psum((proj_piece, squares), "dp")
    loss = squares_all / (row_count * lax.axis_size("dp"))
    return (hidden_acc, grad_proj, loss)


def solution(mesh):
    placed = (P("dp", "fsdp"), P("dp", "fsdp"), P("fsdp", None))
    return jax.shard_map(
        body,
        mesh=mesh,
        in_specs=placed,
        out_specs=(P("dp", "fsdp"), P("fsdp", None), P()),
        check_vma=False,
    )
```

profile of v0, /device:TPU:8, one launch (start us, length us, event | category | flops | bytes accessed | tf_op | source)
XLA Modules:
  0.0 944.8 jit_solution(3194999770944170075)
XLA Ops:
  7.2 0.0 copy-start
  7.2 0.0 copy-start.3
  7.2 0.0 reduce-scatter.2.cloned.1.call-start
  7.2 0.9 copy-done
  8.1 1.9 fusion.12
  10.0 0.0 reduce-scatter.2.cloned.1.call-update
  10.1 0.0 all-gather.2.cloned.1.call-start
  10.1 0.9 fusion.1
  11.1 229.4 %reduce-scatter.2.cloned.1.call-done = f32[96,128]{1,0:T(8,128)} async-done(((f32[1536,128]{1,0:T(8,128)}), f32[96,128]{1,0:T(8,128)}) %reduce-scatter.2.cloned.1.call-update) | async-done | bytes 49168 | tf_op jit(solution)/shard_map/reduce_scatter | solution.py:20
  240.5 0.8 multiply_reduce_fusion.1
  241.3 47.7 %all-reduce = (f32[128]{0:T(128)S(1)}, f32[128]{0:T(128)S(1)}) all-reduce(f32[128]{0:T(128)S(1)} %multiply_reduce_fusion.1, f32[128]{0:T(128)S(1)} %fusion.1), channel_id=1, replica_groups=mesh['dp'=32,'fsdp'=16] {'fsdp'}, use_global_device_ids=true, to_apply=%region_2.0 | all-reduce | flops 256 | bytes 2048 | tf_op jit(solution)/shard_map/psum | solution.py:27
  289.0 0.8 bitcast_convert_fusion
  289.8 0.1 copy.6
  289.9 0.0 copy-done.3
  289.9 0.1 fusion.10
  290.0 0.7 pad_maximum_fusion
  290.8 0.0 all-gather.2.cloned.1.call-update
  290.8 0.0 all-reduce.4.cloned.1.call-start
  290.9 61.7 %all-gather.2.cloned.1.call-done = bf16[4096,352]{1,0:T(8,128)(2,1)} async-done(((bf16[128,352]{1,0:T(8,128)(2,1)}), bf16[4096,352]{1,0:T(8,128)(2,1)}) %all-gather.2.cloned.1.call-update) | async-done | bytes 2883600 | tf_op jit(solution)/shard_map/all_gather | solution.py:36
  352.6 4.4 fusion.3
  357.0 0.0 copy-start.2
  357.0 0.0 all-reduce.4.cloned.1.call-update
  357.1 0.0 copy-start.4
  357.1 0.0 all-reduce.6.cloned.1.call-start
  357.1 205.8 %all-reduce.4.cloned.1.call-done = f32[128,4096]{1,0:T(8,128)} async-done(((f32[128,4096]{1,0:T(8,128)}), f32[128,4096]{1,0:T(8,128)}) %all-reduce.4.cloned.1.call-update) | async-done | bytes 2097168 | tf_op jit(solution)/shard_map/psum | solution.py:38
  562.9 0.0 copy-done.2
  562.9 0.0 copy-start.1
  562.9 3.5 fusion.5
  566.3 48.1 %psum.45 = f32[128]{0:T(128)S(1)} all-reduce(f32[128]{0:T(128)S(1)} %get-tuple-element.7), channel_id=1, replica_groups=mesh['dp'=32,'fsdp'=16] {'fsdp'}, use_global_device_ids=true, to_apply=%region_7.0 | all-reduce | flops 128 | bytes 1024 | tf_op jit(solution)/shard_map/psum | solution.py:11
  614.4 53.8 %all_gather.7 = bf16[128,1536]{0,1:T(8,128)(2,1)S(1)} all-gather(bf16[128,96]{0,1:T(8,128)(2,1)S(1)} %fusion.8), channel_id=1, replica_groups=mesh['dp'=32,'fsdp'=16] {'fsdp'}, dimensions={1}, use_global_device_ids=true | all-gather | bytes 417792 | tf_op jit(solution)/shard_map/all_gather | solution.py:48
  668.2 0.0 copy-done.4
  668.2 1.1 convolution_bitcast_fusion
  669.3 0.0 all-reduce.6.cloned.1.call-update
  669.3 0.0 copy-done.1
  669.3 1.1 multiply_reduce_fusion
  670.5 68.0 %psum.47 = f32[]{:T(128)} all-reduce(f32[]{:T(128)} %multiply_reduce_fusion), channel_id=1, replica_groups=mesh['dp'=32,'fsdp'=16] {'dp'}, use_global_device_ids=true, to_apply=%region_10.0 | all-reduce | flops 1 | bytes 8 | tf_op jit(solution)/shard_map/psum | solution.py:51
  739.2 0.9 fusion.13
  740.0 195.2 %all-reduce.6.cloned.1.call-done = f32[96,1536]{1,0:T(8,128)} async-done(((f32[96,1536]{1,0:T(8,128)}), f32[96,1536]{1,0:T(8,128)}) %all-reduce.6.cloned.1.call-update) | async-done | bytes 589840 | tf_op jit(solution)/shard_map/psum | solution.py:51
  935.2 1.9 copy.10
  (2 shorter events, 0.0 us)
Async XLA Ops:
  7.2 1.0 copy-start
  7.2 282.8 %copy-start.3 = (bf16[128,256]{1,0:T(8,128)(2,1)S(1)}, bf16[128,256]{1,0:T(8,128)(2,1)}, u32[]{:S(2)}) copy-start(bf16[128,256]{1,0:T(8,128)(2,1)} %param.4) | copy-start | bytes 196612
  7.2 233.3 %reduce-scatter.2.cloned.1.call-start = ((), (), s32[]{:S(2)}) async-start(), calls=%async_computation.1 | async-start | bytes 835584 | tf_op jit(solution)/shard_map/reduce_scatter | solution.py:20
  10.1 342.5 %all-gather.2.cloned.1.call-start = ((), (), s32[]{:S(2)}) async-start(), calls=%async_computation.2 | async-start | bytes 3244032 | tf_op jit(solution)/shard_map/all_gather | solution.py:36
  290.8 272.1 %all-reduce.4.cloned.1.call-start = ((), (), s32[]{:S(2)}) async-start(), calls=%async_computation.3 | async-start | bytes 4194304 | tf_op jit(solution)/shard_map/psum | solution.py:38
  357.0 205.8 %copy-start.2 = (f32[96,128]{1,0:T(8,128)S(1)}, f32[96,128]{1,0:T(8,128)}, u32[]{:S(2)}) copy-start(f32[96,128]{1,0:T(8,128)} %reduce-scatter.2.cloned.1.call-done) | copy-start | bytes 147460
  357.1 311.2 %copy-start.4 = (bf16[128,96]{0,1:T(8,128)(2,1)S(1)}, bf16[128,96]{0,1:T(8,128)(2,1)}, u32[]{:S(2)}) copy-start(bf16[128,96]{0,1:T(8,128)(2,1)} %param.3) | copy-start | bytes 73732
  357.1 578.1 %all-reduce.6.cloned.1.call-start = ((), (), s32[]{:S(2)}) async-start(), calls=%async_computation.4 | async-start | bytes 1179648 | tf_op jit(solution)/shard_map/psum | solution.py:51
  562.9 106.5 %copy-start.1 = (f32[128,4096]{1,0:T(8,128)S(1)}, f32[128,4096]{1,0:T(8,128)}, u32[]{:S(2)}) copy-start(f32[128,4096]{1,0:T(8,128)} %all-reduce.4.cloned.1.call-done) | copy-start | bytes 6291460
Sparse Core Ops, SparseCore 0:
  12.5 227.9 reduce-scatter.1
  290.9 61.6 all-gather.1
  357.2 205.6 all-reduce.3
  669.4 265.7 all-reduce.5
where the time goes:
time: 945 us
  waiting for transfers between devices  692 us (73%)
  blocking collectives  218 us (23%)
  between operations  15.6 us (2%)
  matrix products  11.7 us (1%)
    reduce_scatter x1, waiting for transfers between devices, body(): lax.psum_scatter(lax.dot_general(projector, hidden, width_cross, preferre...  229 us
    psum x1, waiting for transfers between devices, body(): differ = lax.psum(partial_value, 'fsdp')  206 us
    psum x1, waiting for transfers between devices, body(): grad_proj, squares_all = lax.psum((proj_piece, squares), 'dp')  195 us
    psum x1, blocking collectives, body(): grad_proj, squares_all = lax.psum((proj_piece, squares), 'dp')  68 us
    all_gather x1, waiting for transfers between devices, body(): lower_all = lax.all_gather(lower, 'dp', axis=0, tiled=True)  61.7 us
    all_gather x1, blocking collectives, body(): piece = lax.all_gather(grad_embed, 'fsdp', axis=1, tiled=True)  53.8 us
    psum x1, blocking collectives, radial_sum(): return lax.psum(jnp.sum(unit_f * grad_unit, axis=1), 'fsdp')  48.1 us
    psum x1, blocking collectives, body(): lax.psum((jnp.sum(embed * embed, axis=1), jnp.sum(teach_f * teach_f, axis...  47.7 us
  transfers between devices with their start and end apart: 4, of which 4 were waited for; matrix products, arithmetic and copies ran while one was open for 0% of the time, Pallas kernels for 0%

commit v1 on v0

--- a/solution.py
+++ b/solution.py
@@ -33,7 +33,9 @@
     target = (teach_f * lax.rsqrt(sq_teacher + EPSILON)[:, None]).astype(jnp.bfloat16)
     upper = jnp.concatenate([student, target], axis=1)
     lower = jnp.concatenate([student, -target], axis=1)
-    lower_all = lax.all_gather(lower, "dp", axis=0, tiled=True)
+    lower_all = jnp.concatenate(
+        lax.all_to_all(jnp.stack([lower] * lax.axis_size("dp")), "dp", 0, 0), axis=0
+    )
     partial_value = lax.dot_general(upper, lower_all, contract, preferred_element_type=jnp.float32)
     differ = lax.psum(partial_value, "fsdp")
     squares = jnp.sum(differ * differ)

time: 945 us -> 950 us (level)
  blocking collectives: 218 us -> 290 us
  waiting for transfers between devices: 692 us -> 625 us
    all_to_all x0 -> x1, blocking collectives: none -> 72.2 us  [body(): lax.all_to_all(jnp.stack([lower] * lax.axis_size('dp')), 'dp', 0, 0)]
    all_gather x1 -> x0, waiting for transfers between devices: 61.7 us -> none  [body(): lower_all = lax.all_gather(lower, 'dp', axis=0, tiled=True)]
  transfers between devices with their start and end apart: 4 -> 3, of which waited for: 4 -> 3; matrix products, arithmetic and copies ran while one was open for 0% -> 1% of each run, Pallas kernels for 0% -> 0%
where the time goes in v1:
time: 950 us
  waiting for transfers between devices  625 us (66%)
  blocking collectives  290 us (31%)
  between operations  15.6 us (2%)
    reduce_scatter x1, waiting for transfers between devices, body(): lax.psum_scatter(lax.dot_general(projector, hidden, width_cross, preferre...  229 us
    psum x1, waiting for transfers between devices, body(): differ = lax.psum(partial_value, 'fsdp')  201 us
    psum x1, waiting for transfers between devices, body(): grad_proj, squares_all = lax.psum((proj_piece, squares), 'dp')  195 us
    all_to_all x1, blocking collectives, body(): lax.all_to_all(jnp.stack([lower] * lax.axis_size('dp')), 'dp', 0, 0)  72.2 us
    psum x1, blocking collectives, body(): grad_proj, squares_all = lax.psum((proj_piece, squares), 'dp')  68.1 us
    all_gather x1, blocking collectives, body(): piece = lax.all_gather(grad_embed, 'fsdp', axis=1, tiled=True)  53.9 us
    psum x1, blocking collectives, radial_sum(): return lax.psum(jnp.sum(unit_f * grad_unit, axis=1), 'fsdp')  48.1 us
    psum x1, blocking collectives, body(): lax.psum((jnp.sum(embed * embed, axis=1), jnp.sum(teach_f * teach_f, axis...  47.7 us
  transfers between devices with their start and end apart: 3, of which 3 were waited for; matrix products, arithmetic and copies ran while one was open for 1% of the time, Pallas kernels for 0%

profile of v1, /device:TPU:8, one launch (start us, length us, event | category | flops | bytes accessed | tf_op | source)
XLA Modules:
  0.0 949.9 jit_solution(17235194168977118549)
XLA Ops:
  7.2 0.0 copy-start
  7.2 0.0 reduce-scatter.2.cloned.1.call-start
  7.2 0.9 copy-done
  8.1 1.9 fusion.12
  10.0 0.0 reduce-scatter.2.cloned.1.call-update
  10.1 0.0 all-reduce.4.cloned.1.call-start
  10.1 0.9 fusion.1
  11.1 229.4 %reduce-scatter.2.cloned.1.call-done = f32[96,128]{1,0:T(8,128)} async-done(((f32[1536,128]{1,0:T(8,128)}), f32[96,128]{1,0:T(8,128)}) %reduce-scatter.2.cloned.1.call-update) | async-done | bytes 49168 | tf_op jit(solution)/shard_map/reduce_scatter | solution.py:20
  240.5 0.8 multiply_reduce_fusion.1
  241.3 47.7 %all-reduce = (f32[128]{0:T(128)S(1)}, f32[128]{0:T(128)S(1)}) all-reduce(f32[128]{0:T(128)S(1)} %multiply_reduce_fusion.1, f32[128]{0:T(128)S(1)} %fusion.1), channel_id=1, replica_groups=mesh['dp'=32,'fsdp'=16] {'fsdp'}, use_global_device_ids=true, to_apply=%region_2.0 | all-reduce | flops 256 | bytes 2048 | tf_op jit(solution)/shard_map/psum | solution.py:27
  289.0 0.8 bitcast_convert_fusion
  289.8 0.1 copy.11
  289.9 0.9 fusion.10
  290.9 0.1 pad_maximum_fusion
  291.0 0.1 copy.13
  291.1 0.4 stack.2
  291.5 72.2 %all_to_all.5 = bf16[32,128,352]{1,2,0:T(8,128)(2,1)S(1)} all-to-all(bf16[32,128,352]{1,2,0:T(8,128)(2,1)S(1)} %stack.2), channel_id=1, replica_groups=mesh['dp'=32,'fsdp'=16] {'dp'}, dimensions={0} | all-to-all | bytes 5767168 | tf_op jit(solution)/shard_map/all_to_all | solution.py:37
  363.7 2.1 fusion.3
  365.8 0.0 all-reduce.4.cloned.1.call-update
  365.8 0.0 copy-start.2
  365.8 0.0 all-reduce.6.cloned.1.call-start
  365.9 1.9 copy_bitcast_fusion
  367.8 0.0 copy-start.3
  367.8 200.8 %all-reduce.4.cloned.1.call-done = f32[128,4096]{1,0:T(8,128)} async-done(((f32[128,4096]{1,0:T(8,128)}), f32[128,4096]{1,0:T(8,128)}) %all-reduce.4.cloned.1.call-update) | async-done | bytes 2097168 | tf_op jit(solution)/shard_map/psum | solution.py:40
  568.6 0.0 copy-done.2
  568.7 0.0 copy-start.1
  568.7 3.2 fusion.5
  571.8 48.1 %psum.45 = f32[128]{0:T(128)S(1)} all-reduce(f32[128]{0:T(128)S(1)} %get-tuple-element.7), channel_id=1, replica_groups=mesh['dp'=32,'fsdp'=16] {'fsdp'}, use_global_device_ids=true, to_apply=%region_7.0 | all-reduce | flops 128 | bytes 1024 | tf_op jit(solution)/shard_map/psum | solution.py:11
  619.9 53.9 %all_gather.3 = bf16[128,1536]{0,1:T(8,128)(2,1)S(1)} all-gather(bf16[128,96]{0,1:T(8,128)(2,1)S(1)} %fusion.8), channel_id=1, replica_groups=mesh['dp'=32,'fsdp'=16] {'fsdp'}, dimensions={1}, use_global_device_ids=true | all-gather | bytes 417792 | tf_op jit(solution)/shard_map/all_gather | solution.py:50
  673.9 0.0 copy-done.3
  673.9 1.1 convolution_bitcast_fusion
  674.9 0.0 all-reduce.6.cloned.1.call-update
  675.0 0.0 copy-done.1
  675.0 1.1 multiply_reduce_fusion
  676.1 68.1 %psum.47 = f32[]{:T(128)} all-reduce(f32[]{:T(128)} %multiply_reduce_fusion), channel_id=1, replica_groups=mesh['dp'=32,'fsdp'=16] {'dp'}, use_global_device_ids=true, to_apply=%region_10.0 | all-reduce | flops 1 | bytes 8 | tf_op jit(solution)/shard_map/psum | solution.py:53
  744.9 0.9 fusion.13
  745.7 194.6 %all-reduce.6.cloned.1.call-done = f32[96,1536]{1,0:T(8,128)} async-done(((f32[96,1536]{1,0:T(8,128)}), f32[96,1536]{1,0:T(8,128)}) %all-reduce.6.cloned.1.call-update) | async-done | bytes 589840 | tf_op jit(solution)/shard_map/psum | solution.py:53
  940.3 1.9 copy.20
  (2 shorter events, 0.0 us)
Async XLA Ops:
  7.2 1.0 copy-start
  7.2 233.3 %reduce-scatter.2.cloned.1.call-start = ((), (), s32[]{:S(2)}) async-start(), calls=%async_computation.2 | async-start | bytes 835584 | tf_op jit(solution)/shard_map/reduce_scatter | solution.py:20
  10.1 558.6 %all-reduce.4.cloned.1.call-start = ((), (), s32[]{:S(2)}) async-start(), calls=%async_computation.3 | async-start | bytes 4194304 | tf_op jit(solution)/shard_map/psum | solution.py:40
  365.8 202.8 %copy-start.2 = (f32[96,128]{1,0:T(8,128)S(1)}, f32[96,128]{1,0:T(8,128)}, u32[]{:S(2)}) copy-start(f32[96,128]{1,0:T(8,128)} %reduce-scatter.2.cloned.1.call-done) | copy-start | bytes 147460
  365.8 574.5 %all-reduce.6.cloned.1.call-start = ((), (), s32[]{:S(2)}) async-start(), calls=%async_computation.4 | async-start | bytes 1179648 | tf_op jit(solution)/shard_map/psum | solution.py:53
  367.8 306.0 %copy-start.3 = (bf16[128,96]{0,1:T(8,128)(2,1)S(1)}, bf16[128,96]{0,1:T(8,128)(2,1)}, u32[]{:S(2)}) copy-start(bf16[128,96]{0,1:T(8,128)(2,1)} %param.3) | copy-start | bytes 73732
  568.7 106.3 %copy-start.1 = (f32[128,4096]{1,0:T(8,128)S(1)}, f32[128,4096]{1,0:T(8,128)}, u32[]{:S(2)}) copy-start(f32[128,4096]{1,0:T(8,128)} %all-reduce.4.cloned.1.call-done) | copy-start | bytes 6291460
Sparse Core Ops, SparseCore 0:
  12.5 227.9 reduce-scatter.1
  366.0 202.6 all-reduce.3
  675.1 265.1 all-reduce.5

commit v2 on v0

--- a/solution.py
+++ b/solution.py
@@ -35,7 +35,7 @@
     lower = jnp.concatenate([student, -target], axis=1)
     lower_all = lax.all_gather(lower, "dp", axis=0, tiled=True)
     partial_value = lax.dot_general(upper, lower_all, contract, preferred_element_type=jnp.float32)
-    differ = lax.psum(partial_value, "fsdp")
+    differ = jnp.sum(lax.all_gather(partial_value, "fsdp"), axis=0)
     squares = jnp.sum(differ * differ)
     grad_unit = 4.0 * jnp.dot(
         differ,

time: 945 us -> 1380 us (1.46)
  waiting for transfers between devices: 692 us -> 1120 us
    all_gather x0 -> x1, waiting for transfers between devices: none -> 627 us  [body(): differ = jnp.sum(lax.all_gather(partial_value, 'fsdp'), axis=0)]
    psum x1 -> x0, waiting for transfers between devices: 206 us -> none  [body(): differ = lax.psum(partial_value, 'fsdp')]
where the time goes in v2:
time: 1380 us
  waiting for transfers between devices  1120 us (81%)
  blocking collectives  213 us (15%)
  other arithmetic  16.3 us (1%)
  between operations  15.6 us (1%)
    all_gather x1, waiting for transfers between devices, body(): differ = jnp.sum(lax.all_gather(partial_value, 'fsdp'), axis=0)  627 us
    reduce_scatter x1, waiting for transfers between devices, body(): lax.psum_scatter(lax.dot_general(projector, hidden, width_cross, preferre...  229 us
    psum x1, waiting for transfers between devices, body(): grad_proj, squares_all = lax.psum((proj_piece, squares), 'dp')  198 us
    psum x1, blocking collectives, body(): grad_proj, squares_all = lax.psum((proj_piece, squares), 'dp')  68.1 us
    all_gather x1, waiting for transfers between devices, body(): lower_all = lax.all_gather(lower, 'dp', axis=0, tiled=True)  61.8 us
    all_gather x1, blocking collectives, body(): piece = lax.all_gather(grad_embed, 'fsdp', axis=1, tiled=True)  49.2 us
    psum x1, blocking collectives, radial_sum(): return lax.psum(jnp.sum(unit_f * grad_unit, axis=1), 'fsdp')  48.2 us
    psum x1, blocking collectives, body(): lax.psum((jnp.sum(embed * embed, axis=1), jnp.sum(teach_f * teach_f, axis...  47.7 us
  transfers between devices with their start and end apart: 4, of which 4 were waited for; matrix products, arithmetic and copies ran while one was open for 0% of the time, Pallas kernels for 0%

profile of v2, /device:TPU:8, one launch (start us, length us, event | category | flops | bytes accessed | tf_op | source)
XLA Modules:
  0.0 1375.6 jit_solution(9857784370625576216)
XLA Ops:
  7.2 0.0 copy-start
  7.2 0.0 copy-start.2
  7.2 0.0 reduce-scatter.2.cloned.1.call-start
  7.2 0.9 copy-done
  8.1 1.9 fusion.12
  10.0 0.0 reduce-scatter.2.cloned.1.call-update
  10.1 0.0 all-gather.4.cloned.1.call-start
  10.1 0.9 fusion.1
  11.1 229.4 %reduce-scatter.2.cloned.1.call-done = f32[96,128]{1,0:T(8,128)} async-done(((f32[1536,128]{1,0:T(8,128)}), f32[96,128]{1,0:T(8,128)}) %reduce-scatter.2.cloned.1.call-update) | async-done | bytes 49168 | tf_op jit(solution)/shard_map/reduce_scatter | solution.py:20
  240.5 0.8 multiply_reduce_fusion.1
  241.3 47.7 %all-reduce = (f32[128]{0:T(128)S(1)}, f32[128]{0:T(128)S(1)}) all-reduce(f32[128]{0:T(128)S(1)} %multiply_reduce_fusion.1, f32[128]{0:T(128)S(1)} %fusion.1), channel_id=1, replica_groups=mesh['dp'=32,'fsdp'=16] {'fsdp'}, use_global_device_ids=true, to_apply=%region_2.0 | all-reduce | flops 256 | bytes 2048 | tf_op jit(solution)/shard_map/psum | solution.py:27
  289.0 0.8 bitcast_convert_fusion
  289.8 0.1 copy.8
  289.9 0.0 copy-done.2
  289.9 0.1 fusion.10
  290.0 0.7 pad_maximum_fusion
  290.8 0.0 all-gather.4.cloned.1.call-update
  290.8 0.0 all-gather.6.cloned.1.call-start
  290.9 61.8 %all-gather.4.cloned.1.call-done = bf16[4096,352]{1,0:T(8,128)(2,1)} async-done(((bf16[128,352]{1,0:T(8,128)(2,1)}), bf16[4096,352]{1,0:T(8,128)(2,1)}) %all-gather.4.cloned.1.call-update) | async-done | bytes 2883600 | tf_op jit(solution)/shard_map/all_gather | solution.py:36
  352.6 4.4 fusion.3
  357.0 0.0 all-gather.6.cloned.1.call-update
  357.1 0.0 all-reduce.3.cloned.1.call-start
  357.1 627.0 %all-gather.6.cloned.1.call-done = f32[2048,4096]{1,0:T(8,128)} async-done(((f32[128,4096]{1,0:T(8,128)}), f32[2048,4096]{1,0:T(8,128)}) %all-gather.6.cloned.1.call-update) | async-done | bytes 33554448 | tf_op jit(solution)/shard_map/all_gather | solution.py:38
  984.1 0.0 copy-start.1
  984.1 11.8 reduce_sum.47
  995.9 0.0 copy-done.1
  995.9 0.0 copy-start.3
  995.9 2.7 fusion.5
  998.6 48.2 %psum.37 = f32[128]{0:T(128)S(1)} all-reduce(f32[128]{0:T(128)S(1)} %get-tuple-element.7), channel_id=1, replica_groups=mesh['dp'=32,'fsdp'=16] {'fsdp'}, use_global_device_ids=true, to_apply=%region_7.0 | all-reduce | flops 128 | bytes 1024 | tf_op jit(solution)/shard_map/psum | solution.py:11
  1046.7 49.2 %all_gather.15 = bf16[128,1536]{0,1:T(8,128)(2,1)S(1)} all-gather(bf16[128,96]{0,1:T(8,128)(2,1)S(1)} %fusion.8), channel_id=1, replica_groups=mesh['dp'=32,'fsdp'=16] {'fsdp'}, dimensions={1}, use_global_device_ids=true | all-gather | bytes 417792 | tf_op jit(solution)/shard_map/all_gather | solution.py:48
  1096.0 0.0 copy-done.3
  1096.0 1.1 convolution_bitcast_fusion
  1097.1 0.0 all-reduce.3.cloned.1.call-update
  1097.1 1.1 multiply_reduce_fusion
  1098.2 68.1 %psum.39 = f32[]{:T(128)} all-reduce(f32[]{:T(128)} %multiply_reduce_fusion), channel_id=1, replica_groups=mesh['dp'=32,'fsdp'=16] {'dp'}, use_global_device_ids=true, to_apply=%region_10.0 | all-reduce | flops 1 | bytes 8 | tf_op jit(solution)/shard_map/psum | solution.py:51
  1167.0 0.9 fusion.13
  1167.8 198.2 %all-reduce.3.cloned.1.call-done = f32[96,1536]{1,0:T(8,128)} async-done(((f32[96,1536]{1,0:T(8,128)}), f32[96,1536]{1,0:T(8,128)}) %all-reduce.3.cloned.1.call-update) | async-done | bytes 589840 | tf_op jit(solution)/shard_map/psum | solution.py:51
  1366.0 1.9 copy.11
  (2 shorter events, 0.0 us)
Async XLA Ops:
  7.2 1.0 copy-start
  7.2 282.8 %copy-start.2 = (bf16[128,256]{1,0:T(8,128)(2,1)S(1)}, bf16[128,256]{1,0:T(8,128)(2,1)}, u32[]{:S(2)}) copy-start(bf16[128,256]{1,0:T(8,128)(2,1)} %param.4) | copy-start | bytes 196612
  7.2 233.3 %reduce-scatter.2.cloned.1.call-start = ((), (), s32[]{:S(2)}) async-start(), calls=%async_computation.1 | async-start | bytes 835584 | tf_op jit(solution)/shard_map/reduce_scatter | solution.py:20
  10.1 342.5 %all-gather.4.cloned.1.call-start = ((), (), s32[]{:S(2)}) async-start(), calls=%async_computation.2 | async-start | bytes 3244032 | tf_op jit(solution)/shard_map/all_gather | solution.py:36
  290.8 693.3 %all-gather.6.cloned.1.call-start = ((), (), s32[]{:S(2)}) async-start(), calls=%async_computation.4 | async-start | bytes 35651584 | tf_op jit(solution)/shard_map/all_gather | solution.py:38
  357.1 1008.9 %all-reduce.3.cloned.1.call-start = ((), (), s32[]{:S(2)}) async-start(), calls=%async_computation.3 | async-start | bytes 1179648 | tf_op jit(solution)/shard_map/psum | solution.py:51
  984.1 11.8 copy-start.1
  995.9 100.1 %copy-start.3 = (bf16[128,96]{0,1:T(8,128)(2,1)S(1)}, bf16[128,96]{0,1:T(8,128)(2,1)}, u32[]{:S(2)}) copy-start(bf16[128,96]{0,1:T(8,128)(2,1)} %param.3) | copy-start | bytes 73732
Sparse Core Ops, SparseCore 0:
  12.5 227.9 reduce-scatter.1
  290.9 61.6 all-gather.3
  357.2 626.8 all-gather.5
  1097.2 268.7 all-reduce.2
